TPU v7x, 256 devices: a whole 4x4x8 slice. The times are simulated.
256 devices in a mesh: row: 8 (over x, z_lo), col: 32 (over z_hi, y, core).
Axes of the slice: x: 4, y: 4, z: 8 (z_hi: 4, z_lo: 2; z = z_hi * 2 + z_lo), core: 2. Of those that a mesh axis runs over, the one named last changes fastest.
Arguments:
- pair: float32 [512, 512, 128], P('row', 'col'), may hold values from -6 to 6
- pair_mask: int32 [512, 512], P('row', 'col'), may hold values from 0 to 1, as said below
- cotangent: float32 [512, 512, 128], P('row', 'col'), may hold values from -6 to 6
- in_gain: float32 [128], replicated, may hold values from 0.25 to 1.75
- in_bias: float32 [128], replicated, may hold values from -2 to 2
- left_weight: bfloat16 [128, 128], replicated, may hold values from -0.5 to 0.5
- left_gate_weight: bfloat16 [128, 128], replicated, may hold values from -0.5 to 0.5
- right_weight: bfloat16 [128, 128], replicated, may hold values from -0.5 to 0.5
- right_gate_weight: bfloat16 [128, 128], replicated, may hold values from -0.5 to 0.5
- out_gain: float32 [128], replicated, may hold values from 0.25 to 1.75
- out_bias: float32 [128], replicated, may hold values from -2 to 2
- output_weight: bfloat16 [128, 128], replicated, may hold values from -0.5 to 0.5
- output_gate_weight: bfloat16 [128, 128], replicated, may hold values from -0.5 to 0.5
Outputs:
- update: float32 [512, 512, 128], P('row', 'col')
- grad_pair: float32 [512, 512, 128], P('row', 'col')
- grad_left: float32 [128, 128], replicated
- grad_left_gate: float32 [128, 128], replicated
- grad_right: float32 [128, 128], replicated
- grad_right_gate: float32 [128, 128], replicated
- grad_output: float32 [128, 128], replicated
- grad_output_gate: float32 [128, 128], replicated
- grad_norms: float32 [4, 128], replicated
Inputs may be any that keep to these rules, and one draw needn't show every extreme that they name: `pair_mask`: pair_mask_ij = r_i * r_j for a 0/1 residue mask r of 512 entries; r holds at least one 0 and at least one 1.
All inputs are finite; a program needn't handle non-finite values.
Results may differ from a plain program's by a relative error of at most 0.0067.
Values may be sent and summed in bfloat16 or wider, within the bound.
A program may use at most 128 MiB of HBM per device.

v0:
```python
import functools

import jax
import jax.numpy as jnp
from jax import lax
from jax.experimental import pallas as pl
from jax.experimental.pallas import tpu as pltpu
from jax.sharding import PartitionSpec as P

EPS = 1e-05
MESH = pl.DeviceIdType.MESH
F32, BF16 = jnp.float32, jnp.bfloat16
X1, P1, P2, X2, P3, X3, P4, X4, A1, A2, A3, A4, A5 = range(13)


def dot(a, b, ca, cb):
    return lax.dot_general(a, b, (((ca,), (cb,)), ((), ())), preferred_element_type=F32)


def swap_halves(a, b):
    low = lax.broadcasted_iota(jnp.int32, a.shape, 1) < 64
    return jnp.where(low, a, pltpu.roll(b, 64, 1)), jnp.where(low, pltpu.roll(a, 64, 1), b)


def kernel(
    pair_in, cot_in, mask_in, gi_in, bi_in, wl_in, wlg_in, wr_in, wrg_in, go_in, bo_in, wo_in, wog_in,
    update_out, grad_pair_out, g_weights_out, g_norms_out,
    update, grad_pair, g_weights, g_norms, xin, cin, pair_mask, in_gain, in_bias, wl, wlg, wr, wrg, out_gain, out_bias, wo, wog, mask, wcat, wcat_t, hat_in, rstd_in, normed, vs, stage, gate, slope, d_out, d_tn, tri_n, tri_f, d_gate, dn, dx,
    cols, acc, give1, send1, got1, lk, rk, rk_t, send2, got2, give2, take2, give3, take3, send3, got3, dt,
    send4, got4, take4, part, a1_give, a1_take, a2_send, a2_got, a3_send, a3_got, a4_send, a4_got, a5_take,
    in_sems, out_sems, ssem, rsem, ready,
):
    row, col = lax.axis_index("row"), lax.axis_index("col")
    cc, q = col // 2, col % 2
    x, zl, zh, y = row // 2, row % 2, cc // 4, cc % 4
    z = zh * 2 + zl
    me = row * 16 + cc
    own = row // 4 == q
    not_own = jnp.logical_not(own)
    chan = (row % 4) * 16 + cc
    plane = x * 4 + y
    sibling = (row, cc * 2 + 1 - q)

    def remote(src, dst, k, dev):
        return pltpu.make_async_remote_copy(
            src_ref=src, dst_ref=dst, send_sem=ssem.at[k], recv_sem=rsem.at[k], device_id=dev, device_id_type=MESH
        )

    def wait_slots(buf, n, sem):
        pltpu.make_async_copy(buf.at[pl.ds(0, n)], buf.at[pl.ds(0, n)], sem).wait()

    far = {0: 2, 1: 1, 2: 3, 3: 0}
    offsets = sorted(((dx, dy) for dx in range(4) for dy in range(4)), key=lambda o: -min(o[0], 4 - o[0]) - min(o[1], 4 - o[1]))
    xs, ys = [(x + d) % 4 for d in range(4)], [(y + d) % 4 for d in range(4)]

    def ring(t):
        return (z + 4 + (1 - 2 * (t % 2)) * ((t + 1) // 2)) % 8

    def at_chip(px, py, pz, fn, index=None):
        prow, pcc = px * 2 + pz % 2, pz // 2 * 4 + py
        fn((prow, pcc * 2 + q), prow * 16 + pcc if index is None else index)

    def each_owner(fn):
        sides = (q * 2 + (x + 1) % 2, q * 2 + x % 2)
        targets = [(side, ys[far[d]]) for d in range(4) for side in sides]

        def send(px, py, pz):
            at_chip(px, py, pz, lambda dev, g: fn(dev, g - 64 * q))

        def step(t, carry):
            pz = ring(t)
            for px, py in targets:
                send(px, py, pz)
            return carry

        lax.fori_loop(0, 7, step, 0)
        for px, py in targets[:-1]:
            send(px, py, z)

        @pl.when(not_own)
        def _():
            send(*targets[-1], z)

    def each_plane(fn):
        for dx, dy in offsets[:-1]:
            at_chip(xs[dx], ys[dy], z, fn, xs[dx] * 4 + ys[dy])

    def each_z(fn):
        def step(t, carry):
            pz = ring(t)
            at_chip(x, y, pz, fn, pz)
            return carry

        lax.fori_loop(0, 7, step, 0)

    def wait_owners(buf, sem):
        @pl.when(own)
        def _():
            wait_slots(buf, 63, sem)

        @pl.when(not_own)
        def _():
            wait_slots(buf, 64, sem)

    def signal(sem, dev):
        pl.semaphore_signal(sem, inc=1, device_id=dev, device_id_type=MESH)

    def cells(ref, s, put=None):
        for h in range(4):
            p, par = h // 2, h % 2
            at = pl.ds(par * 16 + 2 * s + p, 32, stride=32)
            if put is not None:
                ref[at, :] = put[h * 32 : h * 32 + 32]
        if put is None:
            return jnp.concatenate(
                [ref[pl.ds(par * 16 + 2 * s + p, 32, stride=32), :] for p in range(2) for par in range(2)], axis=0
            )

    sources = (pair_in, wl_in, wlg_in, wr_in, wrg_in, mask_in, gi_in, bi_in, go_in, bo_in, wo_in, wog_in, cot_in)
    places = (xin, wl, wlg, wr, wrg, pair_mask, in_gain, in_bias, out_gain, out_bias, wo, wog, cin)
    loads = [pltpu.make_async_copy(a, b, in_sems.at[i]) for i, (a, b) in enumerate(zip(sources, places))]
    for load in loads:
        load.start()
    stores = [
        pltpu.make_async_copy(a, b, out_sems.at[i])
        for i, (a, b) in enumerate(
            ((update, update_out), (grad_pair, grad_pair_out), (g_weights, g_weights_out), (g_norms, g_norms_out))
        )
    ]
    bar = pltpu.get_barrier_semaphore()
    signal(bar, sibling)
    each_z(lambda dev, i: signal(bar, dev))
    each_plane(lambda dev, i: signal(bar, dev))

    for load in loads[1:12]:
        load.wait()
    wcat[...] = jnp.concatenate([wl[...], wlg[...], wr[...], wrg[...]], axis=1)
    for i, w in enumerate((wl, wlg, wr, wrg)):
        wcat_t[i * 128 : i * 128 + 128, :] = w[...].astype(F32).T.astype(BF16)
    cols[0] = jnp.broadcast_to(out_gain[...], (128, 128)).T
    cols[1] = jnp.broadcast_to(out_bias[...], (128, 128)).T
    flags = pair_mask[...].astype(F32)
    laid = jnp.zeros((8, 128), F32)
    for p in range(2):
        pick = lax.broadcasted_iota(jnp.int32, (8, 16), 1) == 2 * lax.broadcasted_iota(jnp.int32, (8, 16), 0) + p
        lane = lax.broadcasted_iota(jnp.int32, (64, 128), 1)
        place = jnp.logical_and(
            lane // 64 == p, lax.broadcasted_iota(jnp.int32, (64, 128), 0) == 2 * (lane % 32) + (lane % 64) // 32
        )
        laid += dot(dot(pick.astype(F32), flags, 1, 0), place.astype(F32), 1, 0)
    mask[...] = laid
    loads[0].wait()

    def project(s, carry):
        v = cells(xin, s)
        center = v - jnp.mean(v, axis=-1, keepdims=True)
        rstd = lax.rsqrt(jnp.mean(center * center, axis=-1, keepdims=True) + EPS)
        hat = center * rstd
        n = (hat * in_gain[...] + in_bias[...]).astype(BF16)
        hat_in[s] = hat
        rstd_in[s] = rstd
        normed[s] = n
        both = dot(wcat_t[...], n, 1, 1)
        m = mask[pl.ds(s, 1), :]
        for side in range(2):
            val = both[side * 256 : side * 256 + 128]
            sig = jax.nn.sigmoid(both[side * 256 + 128 : side * 256 + 256])
            vs[side * 2, s] = val
            vs[side * 2 + 1, s] = sig
            stage[pl.ds(side * 8 + s, 128, stride=16), :] = sig * val * m
        return carry

    lax.fori_loop(0, 4, project, 0)
    pl.semaphore_wait(bar, 23)
    each_plane(lambda dev, i: signal(ready, dev))
    lax.fori_loop(4, 8, project, 0)
    other = pl.multiple_of((1 - q) * 1024, 1024)
    mine = pl.multiple_of(q * 1024, 1024)
    give1[...] = stage[pl.ds(other, 1024), :].reshape(64, 16, 128).astype(BF16)
    send1[:, pl.ds(q, 1)] = stage[pl.ds(mine, 1024), :].reshape(64, 1, 16, 128).astype(BF16)

    x1 = remote(give1, send1.at[:, q], X1, sibling)
    x1.start()
    pl.semaphore_wait(ready, 15)
    x1.wait()
    each_owner(lambda dev, o: remote(send1.at[o], got1.at[me], P1, dev).start())

    @pl.when(own)
    def _():
        got1[pl.ds(me, 1)] = send1[pl.ds(chan, 1)]

    loads[12].wait()

    def gates(s, carry):
        n = normed[s]
        g = jax.nn.sigmoid(dot(n, wog[...], 1, 0))
        ct = cells(cin, s)
        do = (ct * g).astype(BF16)
        gate[s] = g
        slope[s] = ct * g * (1.0 - g)
        d_out[pl.ds(pl.multiple_of(s * 128, 128), 128), :] = do
        d_tn[s] = dot(wo[...], do, 1, 1)
        return carry

    lax.fori_loop(0, 8, gates, 0)

    def by_x(block):
        def step(t, carry):
            block((x + 2 + (1 - 2 * (t % 2)) * ((t + 1) // 2)) % 4)
            return carry

        lax.fori_loop(0, 4, step, 0)

    def send_x(px, fn):
        def step(t, carry):
            pz = ring(t)
            for d in range(4):
                at_chip(px, ys[far[d]], pz, fn)
            return carry

        lax.fori_loop(0, 7, step, 0)
        for d in range(3):
            at_chip(px, ys[far[d]], z, fn)

        @pl.when(px != x)
        def _():
            at_chip(px, y, z, fn)

    @pl.when(own)
    def _():
        wait_slots(got1, 127, rsem.at[P1])
        for rp in range(4):
            a = got1[rp * 32 : rp * 32 + 16].astype(F32)
            b = got1[rp * 32 + 16 : rp * 32 + 32].astype(F32)
            for part_k, dst in ((0, lk), (8, rk)):
                lo, hi = swap_halves(
                    a[:, :, part_k : part_k + 8].reshape(256, 128), b[:, :, part_k : part_k + 8].reshape(256, 128)
                )
                dst[0:256, rp * 128 : rp * 128 + 128] = lo.astype(BF16)
                dst[256:512, rp * 128 : rp * 128 + 128] = hi.astype(BF16)
        rk_t[...] = rk[...].astype(F32).T.astype(BF16)

        def block(px):
            lanes = pl.ds(pl.multiple_of(px * 128, 128), 128)
            v = dot(rk_t[...], lk[:, lanes], 1, 0).reshape(8, 2, 32, 128)
            lo, hi = swap_halves(v[:, 0].reshape(256, 128), v[:, 1].reshape(256, 128))
            send2[pl.ds(px * 32, 16)] = lo.reshape(16, 16, 128).astype(BF16)
            send2[pl.ds(px * 32 + 16, 16)] = hi.reshape(16, 16, 128).astype(BF16)
            send_x(px, lambda dev, t: remote(send2.at[t], got2.at[chan], P2, dev).start())

        by_x(block)
        got2[pl.ds(chan, 1)] = send2[pl.ds(me, 1)]

    wait_owners(got2, rsem.at[P2])

    tri = got2[...].astype(F32)
    first = q == 0
    tri_lo, tri_hi = tri[:, 0:8], tri[:, 8:16]
    give2[...] = jnp.where(first, tri_hi, tri_lo).reshape(32, 16, 128).astype(BF16)
    x2 = remote(give2, take2, X2, sibling)
    x2.start()
    stage[pl.ds(pl.multiple_of(q * 512, 512), 512), :] = jnp.where(first, tri_lo, tri_hi).reshape(512, 128)
    x2.wait()
    stage[pl.ds(pl.multiple_of((1 - q) * 512, 512), 512), :] = take2[...].astype(F32).reshape(512, 128)
    acc[...] = jnp.zeros_like(acc)

    def triangle(s, carry):
        at = pl.ds(s, 128, stride=8)
        t = stage[at, :]
        center = t - jnp.mean(t, axis=0, keepdims=True)
        rstd = lax.rsqrt(jnp.mean(center * center, axis=0, keepdims=True) + EPS)
        hat = center * rstd
        tri_n[s] = (hat * cols[0] + cols[1]).astype(BF16)
        d = d_tn[s]
        dh = d * cols[0]
        mean_dh = jnp.mean(dh, axis=0, keepdims=True)
        mean_dhh = jnp.mean(dh * hat, axis=0, keepdims=True)
        tri_f[at, :] = rstd * (dh - mean_dh - hat * mean_dhh)
        acc[0] += d * hat
        acc[1] += d
        return carry

    lax.fori_loop(0, 8, triangle, 0)
    give3[...] = tri_f[pl.ds(pl.multiple_of((1 - q) * 512, 512), 512), :].reshape(32, 16, 128).astype(BF16)
    x3 = remote(give3, take3, X3, sibling)
    x3.start()
    kept = tri_f[pl.ds(pl.multiple_of(q * 512, 512), 512), :].reshape(64, 8, 128)
    x3.wait()
    came = take3[...].astype(F32).reshape(64, 8, 128)
    send3[...] = jnp.concatenate([jnp.where(first, kept, came), jnp.where(first, came, kept)], axis=1).astype(BF16)
    each_owner(lambda dev, o: remote(send3.at[o], got3.at[me], P3, dev).start())

    @pl.when(own)
    def _():
        got3[pl.ds(me, 1)] = send3[pl.ds(chan, 1)]

    def outputs(s, carry):
        at = pl.ds(pl.multiple_of(s * 128, 128), 128)
        proj = dot(tri_n[s], wo[...], 0, 0)
        cells(update, s, gate[s] * proj)
        dg = (slope[s] * proj).astype(BF16)
        d_gate[at, :] = dg
        dn[s] = dot(dg, wog[...], 1, 1)
        part[512:640, :] += dot(tri_n[s], d_out[at, :], 1, 0)
        part[640:768, :] += dot(normed[s], dg, 0, 0)
        return carry

    part[512:768, :] = jnp.zeros((256, 128), F32)
    lax.fori_loop(0, 8, outputs, 0)
    stores[0].start()

    @pl.when(own)
    def _():
        wait_slots(got3, 127, rsem.at[P3])
        for rp in range(4):
            a = got3[rp * 32 : rp * 32 + 16].astype(F32).reshape(256, 128)
            b = got3[rp * 32 + 16 : rp * 32 + 32].astype(F32).reshape(256, 128)
            lo, hi = swap_halves(a, b)
            dt[:, rp * 128 : rp * 128 + 128] = (
                jnp.concatenate([lo.reshape(8, 1, 32, 128), hi.reshape(8, 1, 32, 128)], axis=1)
                .reshape(512, 128)
                .astype(BF16)
            )

        def block(px):
            lanes = pl.ds(pl.multiple_of(px * 128, 128), 128)
            left = dot(rk[...], dt[:, lanes], 1, 0)
            right = dot(lk[...], dt[lanes, :], 1, 1)
            l_lo, l_hi = swap_halves(left[0:256], left[256:512])
            r_lo, r_hi = swap_halves(right[0:256], right[256:512])
            shape = (16, 2, 8, 128)
            send4[pl.ds(px * 32, 16)] = jnp.concatenate([l_lo.reshape(shape), r_lo.reshape(shape)], axis=2).astype(BF16)
            send4[pl.ds(px * 32 + 16, 16)] = jnp.concatenate(
                [l_hi.reshape(shape), r_hi.reshape(shape)], axis=2
            ).astype(BF16)
            send_x(px, lambda dev, t: remote(send4.at[t], got4.at[chan], P4, dev).start())

        by_x(block)
        got4[pl.ds(chan, 1)] = send4[pl.ds(me, 1)]

    wait_owners(got4, rsem.at[P4])
    x4 = remote(got4.at[:, 1 - q], take4, X4, sibling)
    x4.start()
    stage[pl.ds(mine, 1024), :] = got4[:, pl.ds(q, 1)].astype(F32).reshape(1024, 128)
    x4.wait()
    stage[pl.ds(other, 1024), :] = take4[...].astype(F32).reshape(1024, 128)

    def inward(s, carry):
        m = mask[pl.ds(s, 1), :]
        parts = []
        for side in range(2):
            d = stage[pl.ds(side * 8 + s, 128, stride=16), :] * m
            val, sig = vs[side * 2, s], vs[side * 2 + 1, s]
            parts.append((d * sig).astype(BF16))
            parts.append((d * val * sig * (1.0 - sig)).astype(BF16))
        g = jnp.concatenate(parts, axis=0)
        dx[s] = g
        total = dn[s] + dot(g, wcat[...], 0, 1)
        dn[s] = total
        acc[2] += total * hat_in[s]
        acc[3] += total
        part[0:512, :] += dot(g, normed[s], 1, 0)
        return carry

    part[0:512, :] = jnp.zeros((512, 128), F32)
    lax.fori_loop(0, 8, inward, 0)
    norms = jnp.concatenate(
        [
            jnp.sum(acc[2], axis=0, keepdims=True),
            jnp.sum(acc[3], axis=0, keepdims=True),
            jnp.sum(acc[0].T, axis=0, keepdims=True),
            jnp.sum(acc[1].T, axis=0, keepdims=True),
            jnp.zeros((4, 128), F32),
        ],
        axis=0,
    )

    def half(which):
        return jnp.concatenate(
            [
                part[pl.ds(pl.multiple_of(which * 256, 256), 256), :].reshape(16, 16, 128),
                part[pl.ds(pl.multiple_of(512 + which * 128, 128), 128), :].reshape(16, 8, 128),
                jnp.broadcast_to(norms.reshape(1, 8, 128), (16, 8, 128)),
            ],
            axis=1,
        )

    a1_give[...] = half(1 - q).astype(BF16)
    a1 = remote(a1_give, a1_take, A1, sibling)
    a1.start()
    kept_half = half(q)
    a1.wait()
    a2_send[...] = (kept_half + a1_take[...].astype(F32)).astype(BF16)
    each_plane(lambda dev, i: remote(a2_send.at[i], a2_got.at[plane], A2, dev).start())
    a2_got[pl.ds(plane, 1)] = a2_send[pl.ds(plane, 1)]

    def last(s, carry):
        dhat = dn[s] * in_gain[...]
        hat = hat_in[s]
        mean_d = jnp.mean(dhat, axis=-1, keepdims=True)
        mean_dh = jnp.mean(dhat * hat, axis=-1, keepdims=True)
        cells(grad_pair, s, rstd_in[s] * (dhat - mean_d - hat * mean_dh))
        return carry

    lax.fori_loop(0, 4, last, 0)
    wait_slots(a2_got, 15, rsem.at[A2])
    a3_send[...] = jnp.sum(a2_got[...].astype(F32), axis=0).astype(BF16)
    each_z(lambda dev, i: remote(a3_send, a3_got.at[z], A3, dev).start())
    a3_got[pl.ds(z, 1)] = a3_send[...].reshape(1, 32, 128)
    lax.fori_loop(4, 8, last, 0)
    stores[1].start()
    wait_slots(a3_got, 7, rsem.at[A3])
    total = jnp.sum(a3_got[...].astype(F32), axis=0) * (1.0 / 512.0)
    g_norms[...] = total[24:32]
    a4_send[...] = total.astype(BF16)
    each_plane(lambda dev, i: remote(a4_send, a4_got.at[plane], A4, dev).start())
    a4_got[pl.ds(plane, 1)] = a4_send[...].reshape(1, 32, 128)
    wait_slots(a4_got, 15, rsem.at[A4])
    a5 = remote(a4_got, a5_take, A5, sibling)
    a5.start()
    a5.wait()
    here, there = a4_got[...].astype(F32), a5_take[...].astype(F32)
    for which in range(2):
        piece = jnp.where(q == which, here, there)
        both = piece[:, 0:16].reshape(256, 128)
        g_weights[which * 2] = both[0:128].T
        g_weights[which * 2 + 1] = both[128:256].T
        g_weights[4 + which] = piece[:, 16:24].reshape(128, 128)

    stores[2].start()
    stores[3].start()
    wait_owners(send1, ssem.at[P1])
    wait_owners(send3, ssem.at[P3])

    @pl.when(own)
    def _():
        wait_slots(send2, 127, ssem.at[P2])
        wait_slots(send4, 127, ssem.at[P4])

    wait_slots(a2_send, 15, ssem.at[A2])
    wait_slots(a3_got, 7, ssem.at[A3])
    wait_slots(a4_got, 15, ssem.at[A4])
    for store in stores:
        store.wait()


def hand_out(update, grad_pair, g_weights, g_norms, *refs):
    outs, held, in_sems, sems = refs[:9], refs[9:13], refs[13], refs[14]
    loads = [
        pltpu.make_async_copy(a, b, in_sems.at[i])
        for i, (a, b) in enumerate(zip((update, grad_pair, g_weights, g_norms), held))
    ]
    sources = [held[0], held[1]] + [held[2].at[i] for i in range(6)] + [held[3].at[pl.ds(0, 4)]]
    copies = [pltpu.make_async_copy(a, b, sems.at[i]) for i, (a, b) in enumerate(zip(sources, outs))]
    for load in loads:
        load.start()
    for load, part in zip(loads, (copies[0:1], copies[1:2], copies[2:8], copies[8:9])):
        load.wait()
        for copy in part:
            copy.start()
    for copy in copies:
        copy.wait()


def scratch():
    def v(shape, kind=F32):
        return pltpu.VMEM(shape, kind)

    return [
        v((1024, 128)), v((1024, 128)), v((6, 128, 128)), v((8, 128)),
        v((1024, 128)), v((1024, 128)), v((16, 64), jnp.int32), v((1, 128)), v((1, 128)),
        v((128, 128), BF16), v((128, 128), BF16), v((128, 128), BF16), v((128, 128), BF16),
        v((1, 128)), v((1, 128)), v((128, 128), BF16), v((128, 128), BF16), v((8, 128)),
        v((128, 512), BF16), v((512, 128), BF16),
        v((8, 128, 128)), v((8, 128, 1)), v((8, 128, 128), BF16),
        v((4, 8, 128, 128)), v((2048, 128)),
        v((8, 128, 128)), v((8, 128, 128)), v((1024, 128), BF16),
        v((8, 128, 128)), v((8, 128, 128), BF16), v((1024, 128)),
        v((1024, 128), BF16), v((8, 128, 128)), v((8, 512, 128), BF16),
        v((2, 128, 128)), v((4, 128, 128)),
        v((64, 16, 128), BF16), v((64, 2, 16, 128), BF16), v((128, 2, 16, 128), BF16),
        v((512, 512), BF16), v((512, 512), BF16), v((512, 512), BF16),
        v((128, 16, 128), BF16), v((64, 16, 128), BF16),
        v((32, 16, 128), BF16), v((32, 16, 128), BF16),
        v((32, 16, 128), BF16), v((32, 16, 128), BF16),
        v((64, 16, 128), BF16), v((128, 16, 128), BF16),
        v((512, 512), BF16),
        v((128, 2, 16, 128), BF16), v((64, 2, 16, 128), BF16), v((64, 16, 128), BF16),
        v((768, 128)),
        v((16, 32, 128), BF16), v((16, 32, 128), BF16),
        v((16, 32, 128), BF16), v((16, 32, 128), BF16),
        v((32, 128), BF16), v((8, 32, 128), BF16),
        v((32, 128), BF16), v((16, 32, 128), BF16), v((16, 32, 128), BF16),
        pltpu.SemaphoreType.DMA((13,)),
        pltpu.SemaphoreType.DMA((4,)),
        pltpu.SemaphoreType.DMA((13,)),
        pltpu.SemaphoreType.DMA((13,)),
        pltpu.SemaphoreType.REGULAR,
    ]


def per_device(
    pair, pair_mask, cotangent, in_gain, in_bias, left_weight, left_gate_weight, right_weight, right_gate_weight,
    out_gain, out_bias, output_weight, output_gate_weight,
):
    hbm = pl.BlockSpec(memory_space=pl.ANY)
    square = jax.ShapeDtypeStruct((128, 128), F32)
    cells = jax.ShapeDtypeStruct((1024, 128), F32)
    found = pl.pallas_call(
        kernel,
        out_shape=(cells, cells, jax.ShapeDtypeStruct((6, 128, 128), F32), jax.ShapeDtypeStruct((8, 128), F32)),
        in_specs=[hbm] * 13,
        out_specs=(hbm,) * 4,
        scratch_shapes=scratch(),
        name="triangle",
        compiler_params=pltpu.CompilerParams(
            collective_id=1, has_side_effects=True, vmem_limit_bytes=60 * 1024 * 1024
        ),
    )(
        pair.reshape(1024, 128), cotangent.reshape(1024, 128), pair_mask.T, in_gain.reshape(1, 128), in_bias.reshape(1, 128),
        left_weight, left_gate_weight, right_weight, right_gate_weight,
        out_gain.reshape(1, 128), out_bias.reshape(1, 128), output_weight, output_gate_weight,
    )
    outs = pl.pallas_call(
        hand_out,
        out_shape=(cells, cells) + (square,) * 6 + (jax.ShapeDtypeStruct((4, 128), F32),),
        in_specs=[hbm] * 4,
        out_specs=(hbm,) * 9,
        scratch_shapes=[
            pltpu.VMEM((1024, 128), F32),
            pltpu.VMEM((1024, 128), F32),
            pltpu.VMEM((6, 128, 128), F32),
            pltpu.VMEM((8, 128), F32),
            pltpu.SemaphoreType.DMA((4,)),
            pltpu.SemaphoreType.DMA((9,)),
        ],
        name="hand_out",
        compiler_params=pltpu.CompilerParams(vmem_limit_bytes=60 * 1024 * 1024),
    )(*found)
    return (outs[0].reshape(64, 16, 128), outs[1].reshape(64, 16, 128)) + tuple(outs[2:])


def solution(mesh):
    cell, copied = P("row", "col", None), P()
    return jax.shard_map(
        per_device,
        mesh=mesh,
        in_specs=(cell, P("row", "col"), cell) + (copied,) * 10,
        out_specs=(cell, cell) + (copied,) * 7,
        check_vma=False,
    )
```

profile of v0, /device:TPU:1, one launch (start us, length us, event | category | flops | bytes accessed | tf_op | source)
XLA Modules:
  0.0 94.9 jit_solution(1960827691766541897)
XLA Ops:
  0.6 92.0 %triangle.1 = (f32[1024,128]{1,0:T(8,128)}, f32[1024,128]{1,0:T(8,128)}, f32[6,128,128]{2,1,0:T(8,128)}, f32[8,128]{1,0:T(8,128)}) custom-call(f32[1024,128]{1,0:T(8,128)} %bitcast.9, f32[1024,128]{1,0:T(8,128)} %bitcast.10, s32[16,64]{1,0:T(8,128)} %bitcast.11, f32[1,128]{1,0:T(1,128)} %bitcast.12, f32[1,128]{1,0:T(1,128)} %bitcast.13, ...), custom_call_target="tpu_custom_call" | custom-call | tf_op jit(solution)/shard_map/triangle/pallas_call | solution.py:509
  92.6 2.2 %hand_out.1 = (f32[1024,128]{1,0:T(8,128)}, f32[1024,128]{1,0:T(8,128)}, f32[128,128]{1,0:T(8,128)}, f32[128,128]{1,0:T(8,128)}, f32[128,128]{1,0:T(8,128)}, /*i...) custom-call(f32[1024,128]{1,0:T(8,128)} %get-tuple-element.22.update, ...), custom_call_target="tpu_custom_call" | custom-call | tf_op jit(solution)/shard_map/hand_out/pallas_call | solution.py:524
where the time goes:
time: 95 us; the launch traced here: 94.9 us
  Pallas kernels  94.2 us (99%)
    pallas_call x1, Pallas kernels, per_device(): pl.pallas_call(kernel, out_shape=(cells, cells, jax.ShapeDtypeStruct((6,...  92 us
    pallas_call x1, Pallas kernels, per_device(): pl.pallas_call(hand_out, out_shape=(cells, cells) + (square,) * 6 + (jax....  2.24 us

commit v1 on v0

--- a/solution.py
+++ b/solution.py
@@ -10,7 +10,7 @@
 EPS = 1e-05
 MESH = pl.DeviceIdType.MESH
 F32, BF16 = jnp.float32, jnp.bfloat16
-X1, P1, P2, X2, P3, X3, P4, X4, A1, A2, A3, A4, A5 = range(13)
+X1, X1B, P1, P2, P2B, X2, X2B, P3, X3, X3B, P4, P4B, X4, X4B, A2, A3, A4 = range(17)
 
 
 def dot(a, b, ca, cb):
@@ -27,7 +27,7 @@
     update_out, grad_pair_out, g_weights_out, g_norms_out,
     update, grad_pair, g_weights, g_norms, xin, cin, pair_mask, in_gain, in_bias, wl, wlg, wr, wrg, out_gain, out_bias, wo, wog, mask, wcat, wcat_t, hat_in, rstd_in, normed, vs, stage, gate, slope, d_out, d_tn, tri_n, tri_f, d_gate, dn, dx,
     cols, acc, give1, send1, got1, lk, rk, rk_t, send2, got2, give2, take2, give3, take3, send3, got3, dt,
-    send4, got4, take4, part, a1_give, a1_take, a2_send, a2_got, a3_send, a3_got, a4_send, a4_got, a5_take,
+    send4, got4, take4, part, a2_send, a2_got, a3_send, a3_got, a4_send, a4_got,
     in_sems, out_sems, ssem, rsem, ready,
 ):
     row, col = lax.axis_index("row"), lax.axis_index("col")
@@ -37,7 +37,7 @@
     me = row * 16 + cc
     own = row // 4 == q
     not_own = jnp.logical_not(own)
-    chan = (row % 4) * 16 + cc
+    chan = zl * 32 + x % 2 * 16 + cc
     plane = x * 4 + y
     sibling = (row, cc * 2 + 1 - q)
 
@@ -60,26 +60,47 @@
         prow, pcc = px * 2 + pz % 2, pz // 2 * 4 + py
         fn((prow, pcc * 2 + q), prow * 16 + pcc if index is None else index)
 
-    def each_owner(fn):
+    def by_x(block):
+        def step(t, carry):
+            block((x + 2 + (1 - 2 * (t % 2)) * ((t + 1) // 2)) % 4)
+            return carry
+
+        lax.fori_loop(0, 4, step, 0)
+
+    def send_half(half, fn):
         sides = (q * 2 + (x + 1) % 2, q * 2 + x % 2)
         targets = [(side, ys[far[d]]) for d in range(4) for side in sides]
 
-        def send(px, py, pz):
-            at_chip(px, py, pz, lambda dev, g: fn(dev, g - 64 * q))
-
+        def step(t, carry):
+            pz = (z + 4 + (1 - 2 * (t % 2)) * ((t + 1) // 2) * 2 + (z + half) % 2) % 8
+            for px, py in targets:
+                at_chip(px, py, pz, lambda dev, g: fn(dev, half * 32 + px % 2 * 16 + g % 16))
+            return carry
+
+        lax.fori_loop(0, 3, step, 0)
+        pz = (z + (z + half) % 2) % 8
+        for px, py in targets[:-1]:
+            at_chip(px, py, pz, lambda dev, g: fn(dev, half * 32 + px % 2 * 16 + g % 16))
+
+        @pl.when(jnp.logical_or(not_own, zl != half))
+        def _():
+            px, py = targets[-1]
+            at_chip(px, py, pz, lambda dev, g: fn(dev, half * 32 + px % 2 * 16 + g % 16))
+
+    def send_x(px, fn):
         def step(t, carry):
             pz = ring(t)
-            for px, py in targets:
-                send(px, py, pz)
+            for d in range(4):
+                at_chip(px, ys[far[d]], pz, fn)
             return carry
 
         lax.fori_loop(0, 7, step, 0)
-        for px, py in targets[:-1]:
-            send(px, py, z)
-
-        @pl.when(not_own)
+        for d in range(3):
+            at_chip(px, ys[far[d]], z, fn)
+
+        @pl.when(px != x)
         def _():
-            send(*targets[-1], z)
+            at_chip(px, y, z, fn)
 
     def each_plane(fn):
         for dx, dy in offsets[:-1]:
@@ -101,6 +122,17 @@
         @pl.when(not_own)
         def _():
             wait_slots(buf, 64, sem)
+
+    def wait_half(buf, half, sem):
+        mine_too = jnp.logical_and(own, zl == half)
+
+        @pl.when(mine_too)
+        def _():
+            wait_slots(buf, 31, sem)
+
+        @pl.when(jnp.logical_not(mine_too))
+        def _():
+            wait_slots(buf, 32, sem)
 
     def signal(sem, dev):
         pl.semaphore_signal(sem, inc=1, device_id=dev, device_id_type=MESH)
@@ -132,13 +164,28 @@
     each_z(lambda dev, i: signal(bar, dev))
     each_plane(lambda dev, i: signal(bar, dev))
 
-    for load in loads[1:12]:
+    for load in (loads[0], loads[6], loads[7]):
         load.wait()
-    wcat[...] = jnp.concatenate([wl[...], wlg[...], wr[...], wrg[...]], axis=1)
+
+    def center(s, carry):
+        v = cells(xin, s)
+        middle = v - jnp.mean(v, axis=-1, keepdims=True)
+        rstd = lax.rsqrt(jnp.mean(middle * middle, axis=-1, keepdims=True) + EPS)
+        hat = middle * rstd
+        hat_in[s] = hat
+        rstd_in[s] = rstd
+        normed[s] = (hat * in_gain[...] + in_bias[...]).astype(BF16)
+        return carry
+
+    lax.fori_loop(0, 8, center, 0)
+    for load in loads[1:6] + loads[8:12]:
+        load.wait()
     for i, w in enumerate((wl, wlg, wr, wrg)):
-        wcat_t[i * 128 : i * 128 + 128, :] = w[...].astype(F32).T.astype(BF16)
-    cols[0] = jnp.broadcast_to(out_gain[...], (128, 128)).T
-    cols[1] = jnp.broadcast_to(out_bias[...], (128, 128)).T
+        turned = w[...].astype(F32).T.astype(BF16)
+        for half in range(2):
+            for core in range(2):
+                to = half * 256 + i * 64 + core * 32
+                wcat_t[to : to + 32, :] = turned[core * 64 + half * 32 : core * 64 + half * 32 + 32]
     flags = pair_mask[...].astype(F32)
     laid = jnp.zeros((8, 128), F32)
     for p in range(2):
@@ -149,82 +196,46 @@
         )
         laid += dot(dot(pick.astype(F32), flags, 1, 0), place.astype(F32), 1, 0)
     mask[...] = laid
-    loads[0].wait()
-
-    def project(s, carry):
-        v = cells(xin, s)
-        center = v - jnp.mean(v, axis=-1, keepdims=True)
-        rstd = lax.rsqrt(jnp.mean(center * center, axis=-1, keepdims=True) + EPS)
-        hat = center * rstd
-        n = (hat * in_gain[...] + in_bias[...]).astype(BF16)
-        hat_in[s] = hat
-        rstd_in[s] = rstd
-        normed[s] = n
-        both = dot(wcat_t[...], n, 1, 1)
-        m = mask[pl.ds(s, 1), :]
-        for side in range(2):
-            val = both[side * 256 : side * 256 + 128]
-            sig = jax.nn.sigmoid(both[side * 256 + 128 : side * 256 + 256])
-            vs[side * 2, s] = val
-            vs[side * 2 + 1, s] = sig
-            stage[pl.ds(side * 8 + s, 128, stride=16), :] = sig * val * m
-        return carry
-
-    lax.fori_loop(0, 4, project, 0)
     pl.semaphore_wait(bar, 23)
     each_plane(lambda dev, i: signal(ready, dev))
-    lax.fori_loop(4, 8, project, 0)
+
+    def project(half):
+        def step(s, carry):
+            both = dot(wcat_t[half * 256 : half * 256 + 256, :], normed[s], 1, 1)
+            m = mask[pl.ds(s, 1), :]
+            for side in range(2):
+                val = both[side * 128 : side * 128 + 64]
+                sig = jax.nn.sigmoid(both[side * 128 + 64 : side * 128 + 128])
+                value = sig * val * m
+                for core in range(2):
+                    start = core * 64 + half * 32
+                    rows = slice(core * 32, core * 32 + 32)
+                    vs[side * 2, s, pl.ds(start, 32), :] = val[rows]
+                    vs[side * 2 + 1, s, pl.ds(start, 32), :] = sig[rows]
+                    stage[pl.ds(start * 16 + side * 8 + s, 32, stride=16), :] = value[rows]
+            return carry
+
+        lax.fori_loop(0, 8, step, 0)
+        to = pl.ds(half * 32, 32)
+        theirs = pl.ds(pl.multiple_of((1 - q) * 1024 + half * 512, 512), 512)
+        ours = pl.ds(pl.multiple_of(q * 1024 + half * 512, 512), 512)
+        give1[to] = stage[theirs, :].reshape(32, 16, 128).astype(BF16)
+        send1[to, pl.ds(q, 1)] = stage[ours, :].reshape(32, 1, 16, 128).astype(BF16)
+        copy = remote(give1.at[pl.ds(half * 32, 32)], send1.at[pl.ds(half * 32, 32), q], (X1, X1B)[half], sibling)
+        copy.start()
+        return copy
+
+    x1 = [project(0), project(1)]
     other = pl.multiple_of((1 - q) * 1024, 1024)
     mine = pl.multiple_of(q * 1024, 1024)
-    give1[...] = stage[pl.ds(other, 1024), :].reshape(64, 16, 128).astype(BF16)
-    send1[:, pl.ds(q, 1)] = stage[pl.ds(mine, 1024), :].reshape(64, 1, 16, 128).astype(BF16)
-
-    x1 = remote(give1, send1.at[:, q], X1, sibling)
-    x1.start()
     pl.semaphore_wait(ready, 15)
-    x1.wait()
-    each_owner(lambda dev, o: remote(send1.at[o], got1.at[me], P1, dev).start())
+    for half in range(2):
+        x1[half].wait()
+        send_half(half, lambda dev, c: remote(send1.at[c], got1.at[me], P1, dev).start())
 
     @pl.when(own)
     def _():
         got1[pl.ds(me, 1)] = send1[pl.ds(chan, 1)]
-
-    loads[12].wait()
-
-    def gates(s, carry):
-        n = normed[s]
-        g = jax.nn.sigmoid(dot(n, wog[...], 1, 0))
-        ct = cells(cin, s)
-        do = (ct * g).astype(BF16)
-        gate[s] = g
-        slope[s] = ct * g * (1.0 - g)
-        d_out[pl.ds(pl.multiple_of(s * 128, 128), 128), :] = do
-        d_tn[s] = dot(wo[...], do, 1, 1)
-        return carry
-
-    lax.fori_loop(0, 8, gates, 0)
-
-    def by_x(block):
-        def step(t, carry):
-            block((x + 2 + (1 - 2 * (t % 2)) * ((t + 1) // 2)) % 4)
-            return carry
-
-        lax.fori_loop(0, 4, step, 0)
-
-    def send_x(px, fn):
-        def step(t, carry):
-            pz = ring(t)
-            for d in range(4):
-                at_chip(px, ys[far[d]], pz, fn)
-            return carry
-
-        lax.fori_loop(0, 7, step, 0)
-        for d in range(3):
-            at_chip(px, ys[far[d]], z, fn)
-
-        @pl.when(px != x)
-        def _():
-            at_chip(px, y, z, fn)
 
     @pl.when(own)
     def _():
@@ -246,22 +257,45 @@
             lo, hi = swap_halves(v[:, 0].reshape(256, 128), v[:, 1].reshape(256, 128))
             send2[pl.ds(px * 32, 16)] = lo.reshape(16, 16, 128).astype(BF16)
             send2[pl.ds(px * 32 + 16, 16)] = hi.reshape(16, 16, 128).astype(BF16)
-            send_x(px, lambda dev, t: remote(send2.at[t], got2.at[chan], P2, dev).start())
+            send_x(px, lambda dev, t: remote(send2.at[t], got2.at[chan], P2 + zl, dev).start())
 
         by_x(block)
         got2[pl.ds(chan, 1)] = send2[pl.ds(me, 1)]
 
-    wait_owners(got2, rsem.at[P2])
-
-    tri = got2[...].astype(F32)
+    loads[12].wait()
+    wcat[...] = jnp.concatenate([wl[...], wlg[...], wr[...], wrg[...]], axis=1)
+    cols[0] = jnp.broadcast_to(out_gain[...], (128, 128)).T
+    cols[1] = jnp.broadcast_to(out_bias[...], (128, 128)).T
+
+    def gates(s, carry):
+        n = normed[s]
+        g = jax.nn.sigmoid(dot(n, wog[...], 1, 0))
+        ct = cells(cin, s)
+        do = (ct * g).astype(BF16)
+        gate[s] = g
+        slope[s] = ct * g * (1.0 - g)
+        d_out[pl.ds(pl.multiple_of(s * 128, 128), 128), :] = do
+        d_tn[s] = dot(wo[...], do, 1, 1)
+        return carry
+
+    lax.fori_loop(0, 8, gates, 0)
+
     first = q == 0
-    tri_lo, tri_hi = tri[:, 0:8], tri[:, 8:16]
-    give2[...] = jnp.where(first, tri_hi, tri_lo).reshape(32, 16, 128).astype(BF16)
-    x2 = remote(give2, take2, X2, sibling)
-    x2.start()
-    stage[pl.ds(pl.multiple_of(q * 512, 512), 512), :] = jnp.where(first, tri_lo, tri_hi).reshape(512, 128)
-    x2.wait()
-    stage[pl.ds(pl.multiple_of((1 - q) * 512, 512), 512), :] = take2[...].astype(F32).reshape(512, 128)
+    x2 = []
+    for half in range(2):
+        wait_half(got2, half, rsem.at[(P2, P2B)[half]])
+        tri = got2[half * 32 : half * 32 + 32].astype(F32)
+        tri_lo, tri_hi = tri[:, 0:8], tri[:, 8:16]
+        part2 = pl.ds(half * 16, 16)
+        give2[part2] = jnp.where(first, tri_hi, tri_lo).reshape(16, 16, 128).astype(BF16)
+        x2.append(remote(give2.at[part2], take2.at[part2], (X2, X2B)[half], sibling))
+        x2[half].start()
+        ours = pl.ds(pl.multiple_of(q * 512 + half * 256, 256), 256)
+        stage[ours, :] = jnp.where(first, tri_lo, tri_hi).reshape(256, 128)
+    for half in range(2):
+        x2[half].wait()
+        theirs = pl.ds(pl.multiple_of((1 - q) * 512 + half * 256, 256), 256)
+        stage[theirs, :] = take2[half * 16 : half * 16 + 16].astype(F32).reshape(256, 128)
     acc[...] = jnp.zeros_like(acc)
 
     def triangle(s, carry):
@@ -281,33 +315,25 @@
         return carry
 
     lax.fori_loop(0, 8, triangle, 0)
-    give3[...] = tri_f[pl.ds(pl.multiple_of((1 - q) * 512, 512), 512), :].reshape(32, 16, 128).astype(BF16)
-    x3 = remote(give3, take3, X3, sibling)
-    x3.start()
-    kept = tri_f[pl.ds(pl.multiple_of(q * 512, 512), 512), :].reshape(64, 8, 128)
-    x3.wait()
-    came = take3[...].astype(F32).reshape(64, 8, 128)
-    send3[...] = jnp.concatenate([jnp.where(first, kept, came), jnp.where(first, came, kept)], axis=1).astype(BF16)
-    each_owner(lambda dev, o: remote(send3.at[o], got3.at[me], P3, dev).start())
+    x3 = []
+    for half in range(2):
+        theirs = pl.ds(pl.multiple_of((1 - q) * 512 + half * 256, 256), 256)
+        part3 = pl.ds(half * 16, 16)
+        give3[part3] = tri_f[theirs, :].reshape(16, 16, 128).astype(BF16)
+        x3.append(remote(give3.at[part3], take3.at[part3], (X3, X3B)[half], sibling))
+        x3[half].start()
+    for half in range(2):
+        kept = tri_f[pl.ds(pl.multiple_of(q * 512 + half * 256, 256), 256), :].reshape(32, 8, 128)
+        x3[half].wait()
+        came = take3[pl.ds(half * 16, 16)].astype(F32).reshape(32, 8, 128)
+        send3[pl.ds(half * 32, 32)] = jnp.concatenate(
+            [jnp.where(first, kept, came), jnp.where(first, came, kept)], axis=1
+        ).astype(BF16)
+        send_half(half, lambda dev, c: remote(send3.at[c], got3.at[me], P3, dev).start())
 
     @pl.when(own)
     def _():
         got3[pl.ds(me, 1)] = send3[pl.ds(chan, 1)]
-
-    def outputs(s, carry):
-        at = pl.ds(pl.multiple_of(s * 128, 128), 128)
-        proj = dot(tri_n[s], wo[...], 0, 0)
-        cells(update, s, gate[s] * proj)
-        dg = (slope[s] * proj).astype(BF16)
-        d_gate[at, :] = dg
-        dn[s] = dot(dg, wog[...], 1, 1)
-        part[512:640, :] += dot(tri_n[s], d_out[at, :], 1, 0)
-        part[640:768, :] += dot(normed[s], dg, 0, 0)
-        return carry
-
-    part[512:768, :] = jnp.zeros((256, 128), F32)
-    lax.fori_loop(0, 8, outputs, 0)
-    stores[0].start()
 
     @pl.when(own)
     def _():
@@ -333,18 +359,38 @@
             send4[pl.ds(px * 32 + 16, 16)] = jnp.concatenate(
                 [l_hi.reshape(shape), r_hi.reshape(shape)], axis=2
             ).astype(BF16)
-            send_x(px, lambda dev, t: remote(send4.at[t], got4.at[chan], P4, dev).start())
+            send_x(px, lambda dev, t: remote(send4.at[t], got4.at[chan], P4 + zl, dev).start())
 
         by_x(block)
         got4[pl.ds(chan, 1)] = send4[pl.ds(me, 1)]
 
-    wait_owners(got4, rsem.at[P4])
-    x4 = remote(got4.at[:, 1 - q], take4, X4, sibling)
-    x4.start()
-    stage[pl.ds(mine, 1024), :] = got4[:, pl.ds(q, 1)].astype(F32).reshape(1024, 128)
-    x4.wait()
-    stage[pl.ds(other, 1024), :] = take4[...].astype(F32).reshape(1024, 128)
-
+    def outputs(s, carry):
+        at = pl.ds(pl.multiple_of(s * 128, 128), 128)
+        proj = dot(tri_n[s], wo[...], 0, 0)
+        cells(update, s, gate[s] * proj)
+        dg = (slope[s] * proj).astype(BF16)
+        d_gate[at, :] = dg
+        dn[s] = dot(dg, wog[...], 1, 1)
+        part[512:640, :] += dot(tri_n[s], d_out[at, :], 1, 0)
+        part[640:768, :] += dot(normed[s], dg, 0, 0)
+        return carry
+
+    part[512:768, :] = jnp.zeros((256, 128), F32)
+    lax.fori_loop(0, 8, outputs, 0)
+    stores[0].start()
+
+    x4 = []
+    for half in range(2):
+        wait_half(got4, half, rsem.at[(P4, P4B)[half]])
+        part4 = pl.ds(half * 32, 32)
+        x4.append(remote(got4.at[part4, 1 - q], take4.at[part4], (X4, X4B)[half], sibling))
+        x4[half].start()
+        ours = pl.ds(pl.multiple_of(q * 1024 + half * 512, 512), 512)
+        stage[ours, :] = got4[part4, pl.ds(q, 1)].astype(F32).reshape(512, 128)
+    for half in range(2):
+        x4[half].wait()
+        theirs = pl.ds(pl.multiple_of((1 - q) * 1024 + half * 512, 512), 512)
+        stage[theirs, :] = take4[half * 32 : half * 32 + 32].astype(F32).reshape(512, 128)
     def inward(s, carry):
         m = mask[pl.ds(s, 1), :]
         parts = []
@@ -375,24 +421,23 @@
         axis=0,
     )
 
-    def half(which):
-        return jnp.concatenate(
+    for which in range(2):
+        a2_send[which * 16 : which * 16 + 16] = jnp.concatenate(
             [
-                part[pl.ds(pl.multiple_of(which * 256, 256), 256), :].reshape(16, 16, 128),
-                part[pl.ds(pl.multiple_of(512 + which * 128, 128), 128), :].reshape(16, 8, 128),
+                part[which * 256 : which * 256 + 256, :].reshape(16, 16, 128),
+                part[512 + which * 128 : 640 + which * 128, :].reshape(16, 8, 128),
                 jnp.broadcast_to(norms.reshape(1, 8, 128), (16, 8, 128)),
             ],
             axis=1,
-        )
-
-    a1_give[...] = half(1 - q).astype(BF16)
-    a1 = remote(a1_give, a1_take, A1, sibling)
-    a1.start()
-    kept_half = half(q)
-    a1.wait()
-    a2_send[...] = (kept_half + a1_take[...].astype(F32)).astype(BF16)
-    each_plane(lambda dev, i: remote(a2_send.at[i], a2_got.at[plane], A2, dev).start())
-    a2_got[pl.ds(plane, 1)] = a2_send[pl.ds(plane, 1)]
+        ).astype(BF16)
+    slot = q * 16 + plane
+
+    def plane_both(fn):
+        each_plane(lambda dev, i: [fn((dev[0], dev[1] // 2 * 2 + core), core * 16 + i) for core in range(2)])
+        fn(sibling, (1 - q) * 16 + plane)
+
+    plane_both(lambda dev, i: remote(a2_send.at[i], a2_got.at[slot], A2, dev).start())
+    a2_got[pl.ds(slot, 1)] = a2_send[pl.ds(slot, 1)]
 
     def last(s, carry):
         dhat = dn[s] * in_gain[...]
@@ -403,7 +448,7 @@
         return carry
 
     lax.fori_loop(0, 4, last, 0)
-    wait_slots(a2_got, 15, rsem.at[A2])
+    wait_slots(a2_got, 31, rsem.at[A2])
     a3_send[...] = jnp.sum(a2_got[...].astype(F32), axis=0).astype(BF16)
     each_z(lambda dev, i: remote(a3_send, a3_got.at[z], A3, dev).start())
     a3_got[pl.ds(z, 1)] = a3_send[...].reshape(1, 32, 128)
@@ -413,15 +458,11 @@
     total = jnp.sum(a3_got[...].astype(F32), axis=0) * (1.0 / 512.0)
     g_norms[...] = total[24:32]
     a4_send[...] = total.astype(BF16)
-    each_plane(lambda dev, i: remote(a4_send, a4_got.at[plane], A4, dev).start())
-    a4_got[pl.ds(plane, 1)] = a4_send[...].reshape(1, 32, 128)
-    wait_slots(a4_got, 15, rsem.at[A4])
-    a5 = remote(a4_got, a5_take, A5, sibling)
-    a5.start()
-    a5.wait()
-    here, there = a4_got[...].astype(F32), a5_take[...].astype(F32)
+    plane_both(lambda dev, i: remote(a4_send, a4_got.at[slot], A4, dev).start())
+    a4_got[pl.ds(slot, 1)] = a4_send[...].reshape(1, 32, 128)
+    wait_slots(a4_got, 31, rsem.at[A4])
     for which in range(2):
-        piece = jnp.where(q == which, here, there)
+        piece = a4_got[which * 16 : which * 16 + 16].astype(F32)
         both = piece[:, 0:16].reshape(256, 128)
         g_weights[which * 2] = both[0:128].T
         g_weights[which * 2 + 1] = both[128:256].T
@@ -434,12 +475,12 @@
 
     @pl.when(own)
     def _():
-        wait_slots(send2, 127, ssem.at[P2])
-        wait_slots(send4, 127, ssem.at[P4])
-
-    wait_slots(a2_send, 15, ssem.at[A2])
+        wait_slots(send2, 127, ssem.at[P2 + zl])
+        wait_slots(send4, 127, ssem.at[P4 + zl])
+
+    wait_slots(a2_send, 31, ssem.at[A2])
     wait_slots(a3_got, 7, ssem.at[A3])
-    wait_slots(a4_got, 15, ssem.at[A4])
+    wait_slots(a4_got, 31, ssem.at[A4])
     for store in stores:
         store.wait()
 
@@ -487,14 +528,13 @@
         v((512, 512), BF16),
         v((128, 2, 16, 128), BF16), v((64, 2, 16, 128), BF16), v((64, 16, 128), BF16),
         v((768, 128)),
-        v((16, 32, 128), BF16), v((16, 32, 128), BF16),
-        v((16, 32, 128), BF16), v((16, 32, 128), BF16),
+        v((32, 32, 128), BF16), v((32, 32, 128), BF16),
         v((32, 128), BF16), v((8, 32, 128), BF16),
-        v((32, 128), BF16), v((16, 32, 128), BF16), v((16, 32, 128), BF16),
+        v((32, 128), BF16), v((32, 32, 128), BF16),
         pltpu.SemaphoreType.DMA((13,)),
         pltpu.SemaphoreType.DMA((4,)),
-        pltpu.SemaphoreType.DMA((13,)),
-        pltpu.SemaphoreType.DMA((13,)),
+        pltpu.SemaphoreType.DMA((17,)),
+        pltpu.SemaphoreType.DMA((17,)),
         pltpu.SemaphoreType.REGULAR,
     ]
 

time: 95 us -> 93.5 us (0.984)
  Pallas kernels: 94.2 us -> 92.7 us
    pallas_call x1, Pallas kernels: 92 us -> 90.5 us  [per_device(): pl.pallas_call(kernel, out_shape=(cells, cells, jax.ShapeDtypeStruct((6,...]
where the time goes in v1:
time: 93.5 us; the launch traced here: 93.4 us
  Pallas kernels  92.7 us (99%)
    pallas_call x1, Pallas kernels, per_device(): pl.pallas_call(kernel, out_shape=(cells, cells, jax.ShapeDtypeStruct((6,...  90.5 us
    pallas_call x1, Pallas kernels, per_device(): pl.pallas_call(hand_out, out_shape=(cells, cells) + (square,) * 6 + (jax....  2.24 us

profile of v1, /device:TPU:1, one launch (start us, length us, event | category | flops | bytes accessed | tf_op | source)
XLA Modules:
  0.0 93.4 jit_solution(18370814868176918538)
XLA Ops:
  0.6 90.5 %triangle.1 = (f32[1024,128]{1,0:T(8,128)}, f32[1024,128]{1,0:T(8,128)}, f32[6,128,128]{2,1,0:T(8,128)}, f32[8,128]{1,0:T(8,128)}) custom-call(f32[1024,128]{1,0:T(8,128)} %bitcast.9, f32[1024,128]{1,0:T(8,128)} %bitcast.10, s32[16,64]{1,0:T(8,128)} %bitcast.11, f32[1,128]{1,0:T(1,128)} %bitcast.12, f32[1,128]{1,0:T(1,128)} %bitcast.13, ...), custom_call_target="tpu_custom_call" | custom-call | tf_op jit(solution)/shard_map/triangle/pallas_call | solution.py:549
  91.1 2.2 %hand_out.1 = (f32[1024,128]{1,0:T(8,128)}, f32[1024,128]{1,0:T(8,128)}, f32[128,128]{1,0:T(8,128)}, f32[128,128]{1,0:T(8,128)}, f32[128,128]{1,0:T(8,128)}, /*i...) custom-call(f32[1024,128]{1,0:T(8,128)} %get-tuple-element.22.update, ...), custom_call_target="tpu_custom_call" | custom-call | tf_op jit(solution)/shard_map/hand_out/pallas_call | solution.py:564

commit v2 on v1

--- a/solution.py
+++ b/solution.py
@@ -24,10 +24,10 @@
 
 def kernel(
     pair_in, cot_in, mask_in, gi_in, bi_in, wl_in, wlg_in, wr_in, wrg_in, go_in, bo_in, wo_in, wog_in,
-    update_out, grad_pair_out, g_weights_out, g_norms_out,
-    update, grad_pair, g_weights, g_norms, xin, cin, pair_mask, in_gain, in_bias, wl, wlg, wr, wrg, out_gain, out_bias, wo, wog, mask, wcat, wcat_t, hat_in, rstd_in, normed, vs, stage, gate, slope, d_out, d_tn, tri_n, tri_f, d_gate, dn, dx,
+    update_out, grad_pair_out, pieces_out, g_norms_out,
+    update, grad_pair, g_norms, xin, cin, pair_mask, in_gain, in_bias, wl, wlg, wr, wrg, out_gain, out_bias, wo, wog, mask, wcat, wcat_t, hat_in, rstd_in, normed, vs, stage, gate, slope, d_out, d_tn, tri_n, tri_f, d_gate, dn, dx,
     cols, acc, give1, send1, got1, lk, rk, rk_t, send2, got2, give2, take2, give3, take3, send3, got3, dt,
-    send4, got4, take4, part, a2_send, a2_got, a3_send, a3_got, a4_send, a4_got,
+    send4, got4, take4, part, a2_send, a2_got, a3_send, a3_got, a4_send, out_norms,
     in_sems, out_sems, ssem, rsem, ready,
 ):
     row, col = lax.axis_index("row"), lax.axis_index("col")
@@ -156,7 +156,7 @@
     stores = [
         pltpu.make_async_copy(a, b, out_sems.at[i])
         for i, (a, b) in enumerate(
-            ((update, update_out), (grad_pair, grad_pair_out), (g_weights, g_weights_out), (g_norms, g_norms_out))
+            ((update, update_out), (grad_pair, grad_pair_out), (a4_send, pieces_out.at[q * 16 + plane]), (g_norms, g_norms_out))
         )
     ]
     bar = pltpu.get_barrier_semaphore()
@@ -378,6 +378,8 @@
     part[512:768, :] = jnp.zeros((256, 128), F32)
     lax.fori_loop(0, 8, outputs, 0)
     stores[0].start()
+    for i in range(2):
+        out_norms[i : i + 1, :] = jnp.sum(acc[i].T, axis=0, keepdims=True)
 
     x4 = []
     for half in range(2):
@@ -414,8 +416,7 @@
         [
             jnp.sum(acc[2], axis=0, keepdims=True),
             jnp.sum(acc[3], axis=0, keepdims=True),
-            jnp.sum(acc[0].T, axis=0, keepdims=True),
-            jnp.sum(acc[1].T, axis=0, keepdims=True),
+            out_norms[...],
             jnp.zeros((4, 128), F32),
         ],
         axis=0,
@@ -458,18 +459,11 @@
     total = jnp.sum(a3_got[...].astype(F32), axis=0) * (1.0 / 512.0)
     g_norms[...] = total[24:32]
     a4_send[...] = total.astype(BF16)
-    plane_both(lambda dev, i: remote(a4_send, a4_got.at[slot], A4, dev).start())
-    a4_got[pl.ds(slot, 1)] = a4_send[...].reshape(1, 32, 128)
-    wait_slots(a4_got, 31, rsem.at[A4])
-    for which in range(2):
-        piece = a4_got[which * 16 : which * 16 + 16].astype(F32)
-        both = piece[:, 0:16].reshape(256, 128)
-        g_weights[which * 2] = both[0:128].T
-        g_weights[which * 2 + 1] = both[128:256].T
-        g_weights[4 + which] = piece[:, 16:24].reshape(128, 128)
-
+    plane_both(lambda dev, i: remote(a4_send, pieces_out.at[slot], A4, dev).start())
     stores[2].start()
     stores[3].start()
+    wait_slots(pieces_out, 31, rsem.at[A4])
+
     wait_owners(send1, ssem.at[P1])
     wait_owners(send3, ssem.at[P3])
 
@@ -480,25 +474,33 @@
 
     wait_slots(a2_send, 31, ssem.at[A2])
     wait_slots(a3_got, 7, ssem.at[A3])
-    wait_slots(a4_got, 31, ssem.at[A4])
+    wait_slots(pieces_out, 31, ssem.at[A4])
     for store in stores:
         store.wait()
 
 
-def hand_out(update, grad_pair, g_weights, g_norms, *refs):
-    outs, held, in_sems, sems = refs[:9], refs[9:13], refs[13], refs[14]
+def hand_out(update, grad_pair, pieces, g_norms, *refs):
+    outs, held, weights, in_sems, sems = refs[:9], refs[9:13], refs[13], refs[14], refs[15]
     loads = [
         pltpu.make_async_copy(a, b, in_sems.at[i])
-        for i, (a, b) in enumerate(zip((update, grad_pair, g_weights, g_norms), held))
+        for i, (a, b) in enumerate(zip((pieces, update, grad_pair, g_norms), held))
     ]
-    sources = [held[0], held[1]] + [held[2].at[i] for i in range(6)] + [held[3].at[pl.ds(0, 4)]]
+    sources = [held[1], held[2]] + [weights.at[i] for i in range(6)] + [held[3].at[pl.ds(0, 4)]]
     copies = [pltpu.make_async_copy(a, b, sems.at[i]) for i, (a, b) in enumerate(zip(sources, outs))]
     for load in loads:
         load.start()
-    for load, part in zip(loads, (copies[0:1], copies[1:2], copies[2:8], copies[8:9])):
+    loads[0].wait()
+    for which in range(2):
+        piece = held[0][which * 16 : which * 16 + 16].astype(F32)
+        both = piece[:, 0:16].reshape(256, 128)
+        weights[which * 2] = both[0:128].T
+        weights[which * 2 + 1] = both[128:256].T
+        weights[4 + which] = piece[:, 16:24].reshape(128, 128)
+        for i in (which * 2, which * 2 + 1, 4 + which):
+            copies[2 + i].start()
+    for load, copy in zip(loads[1:], (copies[0], copies[1], copies[8])):
         load.wait()
-        for copy in part:
-            copy.start()
+        copy.start()
     for copy in copies:
         copy.wait()
 
@@ -508,7 +510,7 @@
         return pltpu.VMEM(shape, kind)
 
     return [
-        v((1024, 128)), v((1024, 128)), v((6, 128, 128)), v((8, 128)),
+        v((1024, 128)), v((1024, 128)), v((8, 128)),
         v((1024, 128)), v((1024, 128)), v((16, 64), jnp.int32), v((1, 128)), v((1, 128)),
         v((128, 128), BF16), v((128, 128), BF16), v((128, 128), BF16), v((128, 128), BF16),
         v((1, 128)), v((1, 128)), v((128, 128), BF16), v((128, 128), BF16), v((8, 128)),
@@ -530,7 +532,7 @@
         v((768, 128)),
         v((32, 32, 128), BF16), v((32, 32, 128), BF16),
         v((32, 128), BF16), v((8, 32, 128), BF16),
-        v((32, 128), BF16), v((32, 32, 128), BF16),
+        v((32, 128), BF16), v((2, 128)),
         pltpu.SemaphoreType.DMA((13,)),
         pltpu.SemaphoreType.DMA((4,)),
         pltpu.SemaphoreType.DMA((17,)),
@@ -548,7 +550,7 @@
     cells = jax.ShapeDtypeStruct((1024, 128), F32)
     found = pl.pallas_call(
         kernel,
-        out_shape=(cells, cells, jax.ShapeDtypeStruct((6, 128, 128), F32), jax.ShapeDtypeStruct((8, 128), F32)),
+        out_shape=(cells, cells, jax.ShapeDtypeStruct((32, 32, 128), BF16), jax.ShapeDtypeStruct((8, 128), F32)),
         in_specs=[hbm] * 13,
         out_specs=(hbm,) * 4,
         scratch_shapes=scratch(),
@@ -567,10 +569,11 @@
         in_specs=[hbm] * 4,
         out_specs=(hbm,) * 9,
         scratch_shapes=[
+            pltpu.VMEM((32, 32, 128), BF16),
             pltpu.VMEM((1024, 128), F32),
             pltpu.VMEM((1024, 128), F32),
+            pltpu.VMEM((8, 128), F32),
             pltpu.VMEM((6, 128, 128), F32),
-            pltpu.VMEM((8, 128), F32),
             pltpu.SemaphoreType.DMA((4,)),
             pltpu.SemaphoreType.DMA((9,)),
         ],

time: 93.5 us -> 92.7 us (level)
  no operation moved by 1% of the time
where the time goes in v2:
time: 92.7 us; the launch traced here: 92.6 us
  Pallas kernels  91.9 us (99%)
    pallas_call x1, Pallas kernels, per_device(): pl.pallas_call(kernel, out_shape=(cells, cells, jax.ShapeDtypeStruct((32,...  89.7 us
    pallas_call x1, Pallas kernels, per_device(): pl.pallas_call(hand_out, out_shape=(cells, cells) + (square,) * 6 + (jax....  2.27 us

profile of v2, /device:TPU:1, one launch (start us, length us, event | category | flops | bytes accessed | tf_op | source)
XLA Modules:
  0.0 92.6 jit_solution(7717995913038032231)
XLA Ops:
  0.6 89.7 %triangle.1 = (f32[1024,128]{1,0:T(8,128)}, f32[1024,128]{1,0:T(8,128)}, bf16[32,32,128]{2,1,0:T(8,128)(2,1)}, f32[8,128]{1,0:T(8,128)}) custom-call(f32[1024,128]{1,0:T(8,128)} %bitcast.9, f32[1024,128]{1,0:T(8,128)} %bitcast.10, s32[16,64]{1,0:T(8,128)} %bitcast.11, f32[1,128]{1,0:T(1,128)} %bitcast.12, f32[1,128]{1,0:T(1,128)} %bitcast.13, ...), custom_call_target="tpu_custom_call" | custom-call | tf_op jit(solution)/shard_map/triangle/pallas_call | solution.py:551
  90.3 2.3 %hand_out.1 = (f32[1024,128]{1,0:T(8,128)}, f32[1024,128]{1,0:T(8,128)}, f32[128,128]{1,0:T(8,128)}, f32[128,128]{1,0:T(8,128)}, f32[128,128]{1,0:T(8,128)}, /*i...) custom-call(f32[1024,128]{1,0:T(8,128)} %get-tuple-element.22.update, ...), custom_call_target="tpu_custom_call" | custom-call | tf_op jit(solution)/shard_map/hand_out/pallas_call | solution.py:566

commit v3 on v2

--- a/solution.py
+++ b/solution.py
@@ -389,20 +389,29 @@
         x4[half].start()
         ours = pl.ds(pl.multiple_of(q * 1024 + half * 512, 512), 512)
         stage[ours, :] = got4[part4, pl.ds(q, 1)].astype(F32).reshape(512, 128)
+    def sides(core):
+        def step(s, carry):
+            m = mask[pl.ds(s, 1), :]
+            rows = pl.ds(pl.multiple_of(core * 64, 64), 64)
+            for side in range(2):
+                d = stage[pl.ds(core * 1024 + side * 8 + s, 64, stride=16), :] * m
+                val, sig = vs[side * 2, s, rows, :], vs[side * 2 + 1, s, rows, :]
+                start = pl.multiple_of(side * 256 + core * 64, 64)
+                dx[s, pl.ds(start, 64), :] = (d * sig).astype(BF16)
+                dx[s, pl.ds(start + 128, 64), :] = (d * val * sig * (1.0 - sig)).astype(BF16)
+            return carry
+
+        lax.fori_loop(0, 8, step, 0)
+
+    sides(q)
     for half in range(2):
         x4[half].wait()
         theirs = pl.ds(pl.multiple_of((1 - q) * 1024 + half * 512, 512), 512)
         stage[theirs, :] = take4[half * 32 : half * 32 + 32].astype(F32).reshape(512, 128)
+    sides(1 - q)
+
     def inward(s, carry):
-        m = mask[pl.ds(s, 1), :]
-        parts = []
-        for side in range(2):
-            d = stage[pl.ds(side * 8 + s, 128, stride=16), :] * m
-            val, sig = vs[side * 2, s], vs[side * 2 + 1, s]
-            parts.append((d * sig).astype(BF16))
-            parts.append((d * val * sig * (1.0 - sig)).astype(BF16))
-        g = jnp.concatenate(parts, axis=0)
-        dx[s] = g
+        g = dx[s]
         total = dn[s] + dot(g, wcat[...], 0, 1)
         dn[s] = total
         acc[2] += total * hat_in[s]

time: 92.7 us -> 92.6 us (level)
  no operation moved by 1% of the time
where the time goes in v3:
time: 92.6 us; the launch traced here: 92.5 us
  Pallas kernels  91.8 us (99%)
    pallas_call x1, Pallas kernels, per_device(): pl.pallas_call(kernel, out_shape=(cells, cells, jax.ShapeDtypeStruct((32,...  89.6 us
    pallas_call x1, Pallas kernels, per_device(): pl.pallas_call(hand_out, out_shape=(cells, cells) + (square,) * 6 + (jax....  2.27 us

profile of v3, /device:TPU:1, one launch (start us, length us, event | category | flops | bytes accessed | tf_op | source)
XLA Modules:
  0.0 92.5 jit_solution(1755087071956938280)
XLA Ops:
  0.6 89.6 %triangle.1 = (f32[1024,128]{1,0:T(8,128)}, f32[1024,128]{1,0:T(8,128)}, bf16[32,32,128]{2,1,0:T(8,128)(2,1)}, f32[8,128]{1,0:T(8,128)}) custom-call(f32[1024,128]{1,0:T(8,128)} %bitcast.9, f32[1024,128]{1,0:T(8,128)} %bitcast.10, s32[16,64]{1,0:T(8,128)} %bitcast.11, f32[1,128]{1,0:T(1,128)} %bitcast.12, f32[1,128]{1,0:T(1,128)} %bitcast.13, ...), custom_call_target="tpu_custom_call" | custom-call | tf_op jit(solution)/shard_map/triangle/pallas_call | solution.py:560
  90.2 2.3 %hand_out.1 = (f32[1024,128]{1,0:T(8,128)}, f32[1024,128]{1,0:T(8,128)}, f32[128,128]{1,0:T(8,128)}, f32[128,128]{1,0:T(8,128)}, f32[128,128]{1,0:T(8,128)}, /*i...) custom-call(f32[1024,128]{1,0:T(8,128)} %get-tuple-element.22.update, ...), custom_call_target="tpu_custom_call" | custom-call | tf_op jit(solution)/shard_map/hand_out/pallas_call | solution.py:575
